TPU v7x, 128 devices: a whole 4x4x4 slice. The times are simulated.
128 devices in a mesh: dp: 16 (over x, y), expert: 8 (over z, core).
Axes of the slice: x: 4, y: 4, z: 4, core: 2. Of those that a mesh axis runs over, the one named last changes fastest.
Arguments:
- hidden: bfloat16 [16384, 2, 7168], P(('dp', 'expert')), may hold values from -6 to 6
- grad_out: bfloat16 [16384, 2048], P(('dp', 'expert')), may hold values from -6 to 6
- gate_weights: float32 [16384, 2], P(('dp', 'expert')), may hold values from 0.1 to 1
- routes: int32 [16384, 2], P(('dp', 'expert')), may hold values from 0 to 7, all different within a row; in each aligned block of 128 rows (0 to 127, 128 to 255, ...) at most 48 rows name the same one
- example_ids: int32 [16384], P(('dp', 'expert')), may hold values from 0 to 127, as said below
Outputs:
- update: bfloat16 [8, 7168, 2048], P('expert', 'dp')
- norm_ratio: float32 [128], P('dp')
Inputs may be any that keep to these rules, and one draw needn't show every extreme that they name: `routes`: among the 128 tokens of one device no expert is named by more than 48 tokens, and some device reaches 48 for some expert. `example_ids`: ids never fall along the tokens; tokens i * 1024 to (i + 1) * 1024 - 1 hold exactly the examples i * 8 to (i + 1) * 8 - 1, each with one or more tokens.
All inputs are finite; a program needn't handle non-finite values.
Results may differ from a plain program's by a relative error of at most 0.019.
Values may be sent and summed in bfloat16 or wider, within the bound.
A program may use at most 128 MiB of HBM per device.

v0:
```python
import math
import jax
import jax.numpy as jnp
from jax import lax
from jax.sharding import PartitionSpec as P

EX_BLK = 8


def body(hidden, grad_out, gate_weights, routes, example_ids):
    experts = lax.axis_size("expert")
    replicas = lax.axis_size("dp")
    replica = lax.axis_index("dp")
    tokens_here = hidden.shape[0]
    hidden_width = hidden.shape[2]
    out_width = grad_out.shape[1]
    capacity = 3 * tokens_here // experts
    row_count = experts * capacity
    examples = EX_BLK * replicas
    threshold = math.sqrt(hidden_width * out_width * tokens_here * (0.43 + 0.01 * tokens_here))
    grad_rows = (gate_weights[:, :, None] * grad_out[:, None, :].astype(jnp.float32)).astype(
        jnp.bfloat16
    )
    route_flat = routes.reshape(-1)
    chosen = (route_flat[:, None] == jnp.arange(experts, dtype=jnp.int32)[None, :]).astype(
        jnp.int32
    )
    position = jnp.sum((jnp.cumsum(chosen, axis=0) - 1) * chosen, axis=1)
    destin = route_flat * capacity + position
    hidden_sent = (
        jnp.zeros((experts * capacity, hidden_width), jnp.bfloat16)
        .at[destin]
        .set(hidden.reshape(-1, hidden_width))
    )
    grads_sent = (
        jnp.zeros((experts * capacity, out_width), jnp.bfloat16)
        .at[destin]
        .set(grad_rows.reshape(-1, out_width))
    )
    owner_sent = (
        jnp.full((experts * capacity,), -1, jnp.int32).at[destin].set(jnp.repeat(example_ids, 2))
    )
    hidden_in, grads_in, owner_in = (
        lax.all_to_all(
            hidden_sent.reshape(experts, capacity, hidden_width),
            "expert",
            split_axis=0,
            concat_axis=0,
            tiled=True,
        ),
        lax.all_to_all(
            grads_sent.reshape(experts, capacity, out_width),
            "expert",
            split_axis=0,
            concat_axis=0,
            tiled=True,
        ),
        lax.all_to_all(
            owner_sent.reshape(experts, capacity), "expert", split_axis=0, concat_axis=0, tiled=True
        ),
    )
    hidden_in = hidden_in.reshape(row_count, hidden_width)
    grads_in = grads_in.reshape(row_count, out_width)
    owner_in = owner_in.reshape(row_count)
    first_example = replica * EX_BLK
    belongs = (
        owner_in[:, None] == first_example + jnp.arange(EX_BLK, dtype=jnp.int32)[None, :]
    ).astype(jnp.float32)
    hidden_gram = jnp.dot(hidden_in, hidden_in.T, preferred_element_type=jnp.float32)
    grad_gram = jnp.dot(grads_in, grads_in.T, preferred_element_type=jnp.float32)
    matched = (owner_in[:, None] == owner_in[None, :]).astype(jnp.float32)
    row_sums = jnp.sum(hidden_gram * grad_gram * matched, axis=1)
    square_part = jnp.sum(row_sums[:, None] * belongs, axis=0)
    squares = lax.psum(square_part, "expert")
    norm_values = jnp.sqrt(squares)
    factors = jnp.minimum(1.0, threshold / norm_values)
    row_factors = jnp.sum(belongs * factors[None, :], axis=1)
    clipped = (row_factors[:, None] * grads_in.astype(jnp.float32)).astype(jnp.bfloat16)
    shard_width = hidden_width // replicas
    reduced = lax.psum_scatter(
        lax.dot_general(
            hidden_in, clipped, (((0,), (0,)), ((), ())), preferred_element_type=jnp.float32
        ).astype(jnp.bfloat16),
        "dp",
        scatter_dimension=0,
        tiled=True,
    ).astype(jnp.float32)
    update = (reduced / examples).astype(jnp.bfloat16).reshape(1, shard_width, out_width)
    return (update, norm_values / threshold)


def solution(mesh):
    return jax.shard_map(
        body,
        mesh=mesh,
        in_specs=(
            P(("dp", "expert"), None, None),
            P(("dp", "expert"), None),
            P(("dp", "expert"), None),
            P(("dp", "expert"), None),
            P(("dp", "expert")),
        ),
        out_specs=(P("expert", "dp", None), P("dp")),
        check_vma=False,
    )
```

profile of v0, /device:TPU:1, one launch (start us, length us, event | category | flops | bytes accessed | tf_op | source)
XLA Modules:
  0.0 352.0 jit_solution(234594148419169205)
XLA Ops:
  7.2 0.7 broadcast_multiply_fusion
  7.8 0.8 copy.12
  8.6 0.1 eq.57
  8.8 0.1 eq.53
  8.9 0.1 copy.11
  9.0 0.1 mul.75
  9.2 0.6 reduce-window.6
  9.8 0.2 slice_reduce_fusion
  10.0 0.7 broadcast_in_dim.10
  10.8 0.1 reshape.122
  10.9 0.1 fusion.11
  11.0 1.4 scatter_custom_fusion.1
  12.4 0.7 all_to_all.13
  13.1 6.8 %all-to-all-start.1 = ((s32[8,1,48]{2,1,0:T(1,128)}), s32[8,1,48]{2,1,0:T(1,128)S(1)}, u32[]{:S(2)}, u32[]{:S(2)}) async-start(s32[8,1,48]{2,1,0:T(1,128)} %all_to_all.13), calls=%async_computation.1 | async-start | bytes 8192 | tf_op jit(solution)/shard_map/all_to_all | solution.py:58
  19.9 8.4 %reshape.114 = bf16[256,7168]{1,0:T(8,128)(2,1)} reshape(bf16[128,2,7168]{2,1,0:T(2,128)(2,1)} %param.5) | data formatting | bytes 7340032 | tf_op jit(solution)/shard_map/reshape | solution.py:33
  28.3 10.1 %scatter_custom_fusion = bf16[384,7168]{1,0:T(8,128)(2,1)} fusion(s32[256]{0:T(256)S(1)} %bitcast.28, bf16[256,7168]{1,0:T(8,128)(2,1)} %reshape.114, bf16[]{:T(256)} %constant.13.clone.1), kind=kCustom, calls=%fused_computation.6 | custom fusion | bytes 5505536 | tf_op jit(solution)/shard_map/scatter | solution.py:33
  38.4 0.0 all-to-all-done.1
  38.4 0.0 copy-start.1
  38.4 0.0 copy-start
  38.4 4.9 %all-to-all-start = ((bf16[8,48,7168]{2,1,0:T(8,128)(2,1)}), bf16[8,48,7168]{2,1,0:T(8,128)(2,1)}, u32[]{:S(2)}, u32[]{:S(2)}) async-start(bf16[8,48,7168]{2,1,0:T(8,128)(2,1)} %bitcast.24), calls=%async_computation | async-start | bytes 11010048 | tf_op jit(solution)/shard_map/all_to_all | solution.py:44
  43.3 0.0 copy-done.1
  43.3 0.1 copy.14
  43.5 0.1 mul.78
  43.6 0.0 copy-done
  43.6 1.0 mul.80
  44.7 2.5 mul.81
  47.1 4.5 %scatter_custom_fusion.2 = bf16[384,2048]{1,0:T(8,128)(2,1)} fusion(s32[256]{0:T(256)S(1)} %bitcast.29, f32[256,2048]{1,0:T(8,128)} %mul.81, f32[256]{0:T(256)S(1)} %mul.78, bf16[]{:T(256)} %constant.13.clone.1), kind=kCustom, calls=%fused_computation.14 | custom fusion | flops 1048576 | bytes 3671042 | tf_op jit(solution)/shard_map/scatter | solution.py:38
  51.7 54.6 %all-to-all-done = bf16[8,48,7168]{2,1,0:T(8,128)(2,1)} async-done(((bf16[8,48,7168]{2,1,0:T(8,128)(2,1)}), bf16[8,48,7168]{2,1,0:T(8,128)(2,1)}, u32[]{:S(2)}, u32[]{:S(2)}) %all-to-all-start) | async-done | bytes 5505056 | tf_op jit(solution)/shard_map/all_to_all | solution.py:44
  106.3 4.4 %all-to-all-start.2 = ((bf16[8,48,2048]{2,1,0:T(8,128)(2,1)}), bf16[8,48,2048]{2,1,0:T(8,128)(2,1)S(1)}, u32[]{:S(2)}, u32[]{:S(2)}) async-start(bf16[8,48,2048]{2,1,0:T(8,128)(2,1)} %bitcast.6), calls=%async_computation.2 | async-start | bytes 3145728 | tf_op jit(solution)/shard_map/all_to_all | solution.py:51
  110.6 0.0 reduce-scatter.2.cloned.1.call-start
  110.6 0.5 broadcast.104
  111.1 0.7 reduce.5
  111.8 0.1 eq.61
  111.9 8.1 %fusion.15 = f32[384,384]{0,1:T(8,128)S(1)} fusion(bf16[384,7168]{1,0:T(8,128)(2,1)} %bitcast.5), kind=kOutput, calls=%fused_computation.34 | convolution fusion | flops 2113929216 | bytes 6094848 | tf_op jit(solution)/shard_map/dot_general | solution.py:69
  120.0 11.3 %all-to-all-done.2 = bf16[8,48,2048]{2,1,0:T(8,128)(2,1)S(1)} async-done(((bf16[8,48,2048]{2,1,0:T(8,128)(2,1)}), bf16[8,48,2048]{2,1,0:T(8,128)(2,1)S(1)}, u32[]{:S(2)}, u32[]{:S(2)}) %all-to-all-start.2) | async-done | bytes 1572896 | tf_op jit(solution)/shard_map/all_to_all | solution.py:51
  131.4 1.0 fusion.5
  132.4 0.2 fusion.9
  132.6 12.6 %psum.7 = f32[8]{0:T(128)S(1)} all-reduce(f32[8]{0:T(128)S(1)} %fusion.9), channel_id=1, replica_groups=mesh['dp'=16,'expert'=8] {'expert'}, use_global_device_ids=true, to_apply=%region_8.9 | all-reduce | flops 8 | bytes 64 | tf_op jit(solution)/shard_map/psum | solution.py:74
  145.2 0.5 sqrt_multiply_fusion
  145.7 0.1 fusion.10
  145.8 0.1 mul.89
  145.9 22.0 %bitcast_convert_fusion = bf16[7168,2048]{1,0:T(8,128)(2,1)} fusion(bf16[8,48,7168]{2,1,0:T(8,128)(2,1)} %all-to-all-done, bf16[8,48,2048]{2,1,0:T(8,128)(2,1)S(1)} %all-to-all-done.2, f32[8,48]{1,0:T(8,128)S(1)} %mul.89), kind=kOutput, calls=%fused_computation.3 | convolution fusion | flops 11291328512 | bytes 36439552 | tf_op jit(solution)/shard_map/dot_general | solution.py:81
  167.8 0.0 reduce-scatter.2.cloned.1.call-update
  167.9 174.1 %reduce-scatter.2.cloned.1.call-done = bf16[448,2048]{1,0:T(8,128)(2,1)} async-done(((bf16[7168,2048]{1,0:T(8,128)(2,1)}), bf16[448,2048]{1,0:T(8,128)(2,1)}) %reduce-scatter.2.cloned.1.call-update) | async-done | bytes 1835024 | tf_op jit(solution)/shard_map/reduce_scatter | solution.py:80
  341.9 3.2 fusion.2
  (5 shorter events, 0.1 us)
Async XLA Ops:
  13.1 25.3 %all-to-all-start.1 = ((s32[8,1,48]{2,1,0:T(1,128)}), s32[8,1,48]{2,1,0:T(1,128)S(1)}, u32[]{:S(2)}, u32[]{:S(2)}) async-start(s32[8,1,48]{2,1,0:T(1,128)} %all_to_all.13), calls=%async_computation.1 | async-start | bytes 8192 | tf_op jit(solution)/shard_map/all_to_all | solution.py:58
  38.4 5.0 %copy-start.1 = (f32[128,2]{0,1:T(2,128)S(1)}, f32[128,2]{0,1:T(2,128)}, u32[]{:S(2)}) copy-start(f32[128,2]{0,1:T(2,128)} %param.7) | copy-start | bytes 3076
  38.4 5.2 %copy-start = (bf16[128,2048]{1,0:T(8,128)(2,1)S(1)}, bf16[128,2048]{1,0:T(8,128)(2,1)}, u32[]{:S(2)}) copy-start(bf16[128,2048]{1,0:T(8,128)(2,1)} %param.6) | copy-start | bytes 1572868
  38.4 67.9 %all-to-all-start = ((bf16[8,48,7168]{2,1,0:T(8,128)(2,1)}), bf16[8,48,7168]{2,1,0:T(8,128)(2,1)}, u32[]{:S(2)}, u32[]{:S(2)}) async-start(bf16[8,48,7168]{2,1,0:T(8,128)(2,1)} %bitcast.24), calls=%async_computation | async-start | bytes 11010048 | tf_op jit(solution)/shard_map/all_to_all | solution.py:44
  106.3 25.1 %all-to-all-start.2 = ((bf16[8,48,2048]{2,1,0:T(8,128)(2,1)}), bf16[8,48,2048]{2,1,0:T(8,128)(2,1)S(1)}, u32[]{:S(2)}, u32[]{:S(2)}) async-start(bf16[8,48,2048]{2,1,0:T(8,128)(2,1)} %bitcast.6), calls=%async_computation.2 | async-start | bytes 3145728 | tf_op jit(solution)/shard_map/all_to_all | solution.py:51
  110.6 231.3 %reduce-scatter.2.cloned.1.call-start = ((), (), s32[]{:S(2)}) async-start(), calls=%async_computation.4 | async-start | bytes 31195136 | tf_op jit(solution)/shard_map/reduce_scatter | solution.py:80
Sparse Core Ops, SparseCore 0:
  168.0 173.8 reduce-scatter.1
where the time goes:
time: 353 us; the launch traced here: 352 us
  waiting for transfers between devices  240 us (68%)
  matrix products  31.1 us (9%)
  local copies, waits for them, and re-layouts  27.4 us (8%)
  starting transfers between devices  16.1 us (5%)
  between operations  14.1 us (4%)
  blocking collectives  12.6 us (4%)
  other arithmetic  10.6 us (3%)
    reduce_scatter x1, waiting for transfers between devices, body(): lax.psum_scatter(lax.dot_general(hidden_in, clipped, (((0,), (0,)), ((),...  174 us
    all_to_all x1, waiting for transfers between devices, body(): lax.all_to_all(hidden_sent.reshape(experts, capacity, hidden_width), 'exp...  54.6 us
    dot_general x1, matrix products, body(): lax.dot_general(hidden_in, clipped, (((0,), (0,)), ((), ())), preferred_e...  22 us
    psum x1, blocking collectives, body(): squares = lax.psum(square_part, 'expert')  12.6 us
    all_to_all x1, waiting for transfers between devices, body(): lax.all_to_all(grads_sent.reshape(experts, capacity, out_width), 'expert'...  11.3 us
    scatter x1, local copies, waits for them, and re-layouts, body(): hidden_sent = jnp.zeros((experts * capacity, hidden_width), jnp.bfloat16)...  10.1 us
    reshape x1, local copies, waits for them, and re-layouts, body(): hidden.reshape(-1, hidden_width)  8.4 us
    dot_general x1, matrix products, body(): jnp.dot(hidden_in, hidden_in.T, preferred_element_type=jnp.float32)  8.14 us
  transfers between devices with their start and end apart: 4, of which 3 were waited for; matrix products, arithmetic and copies ran while one was open for 10% of the time, Pallas kernels for 0%

commit v1 on v0

--- a/solution.py
+++ b/solution.py
@@ -3,6 +3,7 @@
 import jax.numpy as jnp
 from jax import lax
 from jax.sharding import PartitionSpec as P
+from jax.lax import axis_size, ppermute
 
 EX_BLK = 8
 
@@ -71,7 +72,26 @@
     matched = (owner_in[:, None] == owner_in[None, :]).astype(jnp.float32)
     row_sums = jnp.sum(hidden_gram * grad_gram * matched, axis=1)
     square_part = jnp.sum(row_sums[:, None] * belongs, axis=0)
-    squares = lax.psum(square_part, "expert")
+
+    def _place_vectors(inp):
+        ndev = axis_size("expert")
+
+        def record_guide(carry_in, w2):
+            if w2 >= ndev:
+                return carry_in
+            return record_guide(
+                carry_in
+                + ppermute(
+                    carry_in,
+                    axis_name="expert",
+                    perm=list(map(lambda dd: (dd, dd ^ w2), range(ndev))),
+                ),
+                2 * w2,
+            )
+
+        return record_guide(inp, 1)
+
+    squares = _place_vectors(square_part)
     norm_values = jnp.sqrt(squares)
     factors = jnp.minimum(1.0, threshold / norm_values)
     row_factors = jnp.sum(belongs * factors[None, :], axis=1)

time: 353 us -> 350 us (level)
  blocking collectives: 12.6 us -> 0 us
  waiting for transfers between devices: 240 us -> 248 us
    psum x1 -> x0, blocking collectives: 12.6 us -> none  [body(): squares = lax.psum(square_part, 'expert')]
    ppermute x0 -> x3, waiting for transfers between devices: none -> 6.21 us  [record_guide(): ppermute(carry_in, axis_name='expert', perm=list(map(lambda dd: (dd, dd ^...]
  transfers between devices with their start and end apart: 4 -> 7, of which waited for: 3 -> 6; matrix products, arithmetic and copies ran while one was open for 10% -> 10% of each run, Pallas kernels for 0% -> 0%
where the time goes in v1:
time: 350 us
  waiting for transfers between devices  248 us (71%)
  matrix products  31.1 us (9%)
  local copies, waits for them, and re-layouts  27.4 us (8%)
  starting transfers between devices  18 us (5%)
  between operations  14.1 us (4%)
  other arithmetic  10.6 us (3%)
    reduce_scatter x1, waiting for transfers between devices, body(): lax.psum_scatter(lax.dot_general(hidden_in, clipped, (((0,), (0,)), ((),...  176 us
    all_to_all x1, waiting for transfers between devices, body(): lax.all_to_all(hidden_sent.reshape(experts, capacity, hidden_width), 'exp...  54.6 us
    dot_general x1, matrix products, body(): lax.dot_general(hidden_in, clipped, (((0,), (0,)), ((), ())), preferred_e...  22 us
    all_to_all x1, waiting for transfers between devices, body(): lax.all_to_all(grads_sent.reshape(experts, capacity, out_width), 'expert'...  11.3 us
    scatter x1, local copies, waits for them, and re-layouts, body(): hidden_sent = jnp.zeros((experts * capacity, hidden_width), jnp.bfloat16)...  10.1 us
    reshape x1, local copies, waits for them, and re-layouts, body(): hidden.reshape(-1, hidden_width)  8.4 us
    dot_general x1, matrix products, body(): jnp.dot(hidden_in, hidden_in.T, preferred_element_type=jnp.float32)  8.14 us
  transfers between devices with their start and end apart: 7, of which 6 were waited for; matrix products, arithmetic and copies ran while one was open for 10% of the time, Pallas kernels for 0%

profile of v1, /device:TPU:1, one launch (start us, length us, event | category | flops | bytes accessed | tf_op | source)
XLA Modules:
  0.0 349.6 jit_solution(9516912669223555220)
XLA Ops:
  7.2 0.7 broadcast_multiply_fusion
  7.8 0.8 copy.12
  8.6 0.1 eq.57
  8.8 0.1 eq.53
  8.9 0.1 copy.11
  9.0 0.1 mul.75
  9.2 0.6 reduce-window.6
  9.8 0.2 slice_reduce_fusion
  10.0 0.7 broadcast_in_dim.10
  10.8 0.1 reshape.122
  10.9 0.1 fusion.11
  11.0 1.4 scatter_custom_fusion.1
  12.4 0.7 all_to_all.13
  13.1 6.8 %all-to-all-start.1 = ((s32[8,1,48]{2,1,0:T(1,128)}), s32[8,1,48]{2,1,0:T(1,128)S(1)}, u32[]{:S(2)}, u32[]{:S(2)}) async-start(s32[8,1,48]{2,1,0:T(1,128)} %all_to_all.13), calls=%async_computation.1 | async-start | bytes 8192 | tf_op jit(solution)/shard_map/all_to_all | solution.py:59
  19.9 8.4 %reshape.114 = bf16[256,7168]{1,0:T(8,128)(2,1)} reshape(bf16[128,2,7168]{2,1,0:T(2,128)(2,1)} %param.5) | data formatting | bytes 7340032 | tf_op jit(solution)/shard_map/reshape | solution.py:34
  28.3 10.1 %scatter_custom_fusion = bf16[384,7168]{1,0:T(8,128)(2,1)} fusion(s32[256]{0:T(256)S(1)} %bitcast.28, bf16[256,7168]{1,0:T(8,128)(2,1)} %reshape.114, bf16[]{:T(256)} %constant.13.clone.1), kind=kCustom, calls=%fused_computation.6 | custom fusion | bytes 5505536 | tf_op jit(solution)/shard_map/scatter | solution.py:34
  38.4 0.0 all-to-all-done.1
  38.4 4.9 %all-to-all-start = ((bf16[8,48,7168]{2,1,0:T(8,128)(2,1)}), bf16[8,48,7168]{2,1,0:T(8,128)(2,1)}, u32[]{:S(2)}, u32[]{:S(2)}) async-start(bf16[8,48,7168]{2,1,0:T(8,128)(2,1)} %bitcast.24), calls=%async_computation | async-start | bytes 11010048 | tf_op jit(solution)/shard_map/all_to_all | solution.py:45
  43.3 0.0 copy-done.1
  43.3 0.1 copy.14
  43.5 0.1 mul.78
  43.6 0.0 copy-done
  43.6 1.0 mul.80
  44.7 2.5 mul.81
  47.1 4.5 %scatter_custom_fusion.2 = bf16[384,2048]{1,0:T(8,128)(2,1)} fusion(s32[256]{0:T(256)S(1)} %bitcast.29, f32[256,2048]{1,0:T(8,128)} %mul.81, f32[256]{0:T(256)S(1)} %mul.78, bf16[]{:T(256)} %constant.13.clone.1), kind=kCustom, calls=%fused_computation.14 | custom fusion | flops 1048576 | bytes 3671042 | tf_op jit(solution)/shard_map/scatter | solution.py:39
  51.7 54.6 %all-to-all-done = bf16[8,48,7168]{2,1,0:T(8,128)(2,1)} async-done(((bf16[8,48,7168]{2,1,0:T(8,128)(2,1)}), bf16[8,48,7168]{2,1,0:T(8,128)(2,1)}, u32[]{:S(2)}, u32[]{:S(2)}) %all-to-all-start) | async-done | bytes 5505056 | tf_op jit(solution)/shard_map/all_to_all | solution.py:45
  106.3 4.4 %all-to-all-start.2 = ((bf16[8,48,2048]{2,1,0:T(8,128)(2,1)}), bf16[8,48,2048]{2,1,0:T(8,128)(2,1)S(1)}, u32[]{:S(2)}, u32[]{:S(2)}) async-start(bf16[8,48,2048]{2,1,0:T(8,128)(2,1)} %bitcast.6), calls=%async_computation.2 | async-start | bytes 3145728 | tf_op jit(solution)/shard_map/all_to_all | solution.py:52
  110.6 0.0 reduce-scatter.2.cloned.1.call-start
  110.6 0.5 broadcast.104
  111.1 0.7 reduce.5
  111.8 0.1 eq.61
  111.9 8.1 %fusion.15 = f32[384,384]{0,1:T(8,128)S(1)} fusion(bf16[384,7168]{1,0:T(8,128)(2,1)} %bitcast.5), kind=kOutput, calls=%fused_computation.35 | convolution fusion | flops 2113929216 | bytes 6094848 | tf_op jit(solution)/shard_map/dot_general | solution.py:70
  120.0 11.3 %all-to-all-done.2 = bf16[8,48,2048]{2,1,0:T(8,128)(2,1)S(1)} async-done(((bf16[8,48,2048]{2,1,0:T(8,128)(2,1)}), bf16[8,48,2048]{2,1,0:T(8,128)(2,1)S(1)}, u32[]{:S(2)}, u32[]{:S(2)}) %all-to-all-start.2) | async-done | bytes 1572896 | tf_op jit(solution)/shard_map/all_to_all | solution.py:52
  131.4 1.0 fusion.5
  132.4 0.2 fusion.9
  132.6 1.0 collective-permute-start
  133.5 0.8 collective-permute-done
  134.3 0.3 collective-permute-start.1
  134.6 2.1 collective-permute-done.1
  136.7 0.6 collective-permute-start.2
  137.3 3.3 collective-permute-done.2
  140.6 0.5 broadcast_multiply_fusion.1
  141.1 0.1 fusion.10
  141.2 0.1 mul.89
  141.3 22.0 %bitcast_convert_fusion = bf16[7168,2048]{1,0:T(8,128)(2,1)} fusion(bf16[8,48,7168]{2,1,0:T(8,128)(2,1)} %all-to-all-done, bf16[8,48,2048]{2,1,0:T(8,128)(2,1)S(1)} %all-to-all-done.2, f32[8,48]{1,0:T(8,128)S(1)} %mul.89), kind=kOutput, calls=%fused_computation.3 | convolution fusion | flops 11291328512 | bytes 36439552 | tf_op jit(solution)/shard_map/dot_general | solution.py:101
  163.3 0.0 reduce-scatter.2.cloned.1.call-update
  163.3 176.2 %reduce-scatter.2.cloned.1.call-done = bf16[448,2048]{1,0:T(8,128)(2,1)} async-done(((bf16[7168,2048]{1,0:T(8,128)(2,1)}), bf16[448,2048]{1,0:T(8,128)(2,1)}) %reduce-scatter.2.cloned.1.call-update) | async-done | bytes 1835024 | tf_op jit(solution)/shard_map/reduce_scatter | solution.py:100
  339.5 3.2 fusion.2
  (9 shorter events, 0.1 us)
Async XLA Ops:
  13.1 25.3 %all-to-all-start.1 = ((s32[8,1,48]{2,1,0:T(1,128)}), s32[8,1,48]{2,1,0:T(1,128)S(1)}, u32[]{:S(2)}, u32[]{:S(2)}) async-start(s32[8,1,48]{2,1,0:T(1,128)} %all_to_all.13), calls=%async_computation.1 | async-start | bytes 8192 | tf_op jit(solution)/shard_map/all_to_all | solution.py:59
  38.4 5.0 %copy-start.1 = (f32[128,2]{0,1:T(2,128)S(1)}, f32[128,2]{0,1:T(2,128)}, u32[]{:S(2)}) copy-start(f32[128,2]{0,1:T(2,128)} %param.7) | copy-start | bytes 3076
  38.4 5.2 %copy-start = (bf16[128,2048]{1,0:T(8,128)(2,1)S(1)}, bf16[128,2048]{1,0:T(8,128)(2,1)}, u32[]{:S(2)}) copy-start(bf16[128,2048]{1,0:T(8,128)(2,1)} %param.6) | copy-start | bytes 1572868
  38.4 67.9 %all-to-all-start = ((bf16[8,48,7168]{2,1,0:T(8,128)(2,1)}), bf16[8,48,7168]{2,1,0:T(8,128)(2,1)}, u32[]{:S(2)}, u32[]{:S(2)}) async-start(bf16[8,48,7168]{2,1,0:T(8,128)(2,1)} %bitcast.24), calls=%async_computation | async-start | bytes 11010048 | tf_op jit(solution)/shard_map/all_to_all | solution.py:45
  106.3 25.1 %all-to-all-start.2 = ((bf16[8,48,2048]{2,1,0:T(8,128)(2,1)}), bf16[8,48,2048]{2,1,0:T(8,128)(2,1)S(1)}, u32[]{:S(2)}, u32[]{:S(2)}) async-start(bf16[8,48,2048]{2,1,0:T(8,128)(2,1)} %bitcast.6), calls=%async_computation.2 | async-start | bytes 3145728 | tf_op jit(solution)/shard_map/all_to_all | solution.py:52
  110.6 228.9 %reduce-scatter.2.cloned.1.call-start = ((), (), s32[]{:S(2)}) async-start(), calls=%async_computation.4 | async-start | bytes 31195136 | tf_op jit(solution)/shard_map/reduce_scatter | solution.py:100
  132.6 1.8 collective-permute-start
  134.3 2.4 collective-permute-start.1
  136.7 3.9 %collective-permute-start.2 = (f32[8]{0:T(128)S(1)}, f32[8]{0:T(128)S(1)}, u32[]{:S(2)}, u32[]{:S(2)}) collective-permute-start(f32[8]{0:T(128)S(1)} %add.52), channel_id=1, source_target_pairs={{0,4},{1,5},{2,6},{3,7},{4,0},{5,1},{6,2},{7,3},{8,12},{9,13},{10,... | collective-permute-start | bytes 104 | tf_op jit(solution)/shard_map/ppermute | solution.py:84
Sparse Core Ops, SparseCore 0:
  163.4 176.0 reduce-scatter.1
